TPU v7x, 256 devices: a whole 4x4x8 slice. The times are simulated.
256 devices in a mesh: lat: 32 (over z, y), lon: 8 (over x, core).
Axes of the slice: x: 4, y: 4, z: 8, core: 2. Of those that a mesh axis runs over, the one named last changes fastest.
Arguments:
- grid_fields: bfloat16 [1280, 50, 3, 2560], P('lat', None, None, 'lon'), may hold values from -6 to 6
- legendre: bfloat16 [512, 1280, 640], P(('lat', 'lon')), may hold values from -0.15625 to 0.15625
- wave_of_slot: int32 [512], replicated, may hold values from 0 to 511, as said below
- energy_weight: float32 [3, 640], replicated, may hold values from 0.1 to 10
Outputs:
- spectral: bfloat16 [50, 3, 512, 2, 640], P(None, None, ('lat', 'lon'))
- gram_matrix: float32 [50, 50], replicated
Inputs may be any that keep to these rules, and one draw needn't show every extreme that they name: `wave_of_slot`: every wavenumber 0 to 511 stands in exactly one slot; slot d * 2 + r holds a wavenumber of r * 256 to r * 256 + 255.
All inputs are finite; a program needn't handle non-finite values.
Results may differ from a plain program's by a relative error of at most 0.0043.
Values may be sent and summed in bfloat16 or wider, within the bound.
A program may use at most 128 MiB of HBM per device.

v0:
```python
import math

import jax
import jax.numpy as jnp
from jax import lax
from jax.experimental import pallas as pl
from jax.experimental.pallas import tpu as pltpu
from jax.sharding import PartitionSpec as P

NLON = 2560
M = 512
NT = 640
LEV = 3
F32 = jnp.float32
BF16 = jnp.bfloat16
MESH = pl.DeviceIdType.MESH

FG = 25
CHUNKS = tuple((g, 1) for g in range(6))
SIN_COEF = tuple(
    (-1) ** i * (math.pi / 2) ** (2 * i + 1) / math.factorial(2 * i + 1) for i in range(6)
)


def quarter_sine(z):
    square = z * z
    total = jnp.full_like(z, SIN_COEF[5])
    for coef in SIN_COEF[4::-1]:
        total = total * square + coef
    return total * z


def nt_dot(a, b, precision=None):
    return lax.dot_general(
        a, b, (((1,), (1,)), ((), ())), preferred_element_type=F32, precision=precision
    )


def kernel(
    x_hbm, leg_hbm, wq_ref, wave_ref, ew_ref, spec_ref, gram_ref,
    xv, x32, xs, xrs, xa, xrr, trig, wn, w32, sb, zb, r32, rbs, rb, leg_v, leg32, legp,
    c32, ext32, amat, out, ost, wts, spec_v, gs, ga, gb, gc,
    x_sem, leg_sem, spec_sem, own_sem, s1_send, s1_recv, s1r_send, s1r_recv,
    zy_send, zy_recv, s2_send, s2_recv, g_send, g_recv,
):
    lat = lax.axis_index("lat")
    lon = lax.axis_index("lon")

    def load_x(g):
        rows = pl.ds(FG * g, FG)
        return pltpu.make_async_copy(x_hbm.at[rows], xv.at[rows], x_sem.at[g])

    for g in range(6):
        load_x(g).start()
    leg_copy = pltpu.make_async_copy(leg_hbm, leg_v, leg_sem)
    leg_copy.start()

    barrier = pltpu.get_barrier_semaphore()

    @pl.loop(1, 8)
    def _(k):
        pl.semaphore_signal(
            barrier, inc=1, device_id=(lat, lax.rem(lon + k, 8)), device_id_type=MESH
        )

    @pl.loop(1, 32)
    def _(k):
        pl.semaphore_signal(
            barrier, inc=1, device_id=(lax.rem(lat + k, 32), lon), device_id_type=MESH
        )

    x32[:, :, 1000:1008, :] = jnp.zeros((6, 3, 8, 128), F32)
    ext32[128:136, :] = jnp.zeros((8, 256), F32)

    def relay(g):
        load_x(g).wait()

        @pl.loop(0, FG)
        def _(u):
            rows = xv[FG * g + u].astype(F32)
            for t in range(3):
                width = 128 if t < 2 else 64
                x32[g, t, pl.ds(u, 40, stride=FG), 0:width] = rows[
                    :, t * 128:t * 128 + width
                ]

    def main_copy(c, peer):
        first, count = CHUNKS[c]
        rows = pl.ds(first * 128, count * 128)
        return pltpu.make_async_remote_copy(
            src_ref=xs.at[peer, rows],
            dst_ref=xa.at[rows, pl.ds(pl.multiple_of(lon * 256, 256), 256)],
            send_sem=s1_send, recv_sem=s1_recv.at[c],
            device_id=(lat, peer), device_id_type=MESH,
        )

    def rest_copy(c, peer):
        first, count = CHUNKS[c]
        rows = pl.ds(first * 64, count * 64)
        return pltpu.make_async_remote_copy(
            src_ref=xrs.at[peer, rows], dst_ref=xrr.at[lon, rows],
            send_sem=s1r_send, recv_sem=s1r_recv.at[c],
            device_id=(lat, peer), device_id_type=MESH,
        )

    low = lax.broadcasted_iota(jnp.int32, (64, 128), 1) < 64

    def pack(c, peer):
        first, count = CHUNKS[c]
        for g in range(first, first + count):
            for t in range(2):
                xs[peer, g * 128:(g + 1) * 128, t * 128:(t + 1) * 128] = x32[
                    g, t, pl.ds(peer * 125, 128), :
                ].astype(BF16)
            rest = x32[g, 2, pl.ds(peer * 125, 128), :]
            rest = jnp.where(low, rest[0:64], pltpu.roll(rest[64:128], 64, 1))
            xrs[peer, g * 64:(g + 1) * 64, :] = rest.astype(BF16)

    def own_copy(c):
        first, count = CHUNKS[c]
        rows = pl.ds(first * 128, count * 128)
        return pltpu.make_async_copy(
            xs.at[lon, rows],
            xa.at[rows, pl.ds(pl.multiple_of(lon * 256, 256), 256)],
            own_sem.at[c],
        )

    for c, (first, count) in enumerate(CHUNKS):
        for g in range(first, first + count):
            relay(g)
        if c == 0:
            pl.semaphore_wait(barrier, 38)

        @pl.loop(1, 8)
        def _(k):
            peer = lax.rem(lon + k, 8)
            pack(c, peer)
            main_copy(c, peer).start()
            rest_copy(c, peer).start()

    for c, (first, count) in enumerate(CHUNKS):
        pack(c, lon)
        own_copy(c).start()
        for g in range(first, first + count):
            xrr[lon, g * 64:(g + 1) * 64, :] = xrs[lon, g * 64:(g + 1) * 64, :]

    lane = lax.broadcasted_iota(jnp.int32, (1, 128), 1)
    for b in range(4):
        wn[b * 128:(b + 1) * 128, :] = jnp.transpose(
            jnp.broadcast_to(wq_ref[b:b + 1, :].astype(F32), (128, 128))
        )

    @pl.loop(0, 32)
    def _(z):
        for r in range(2):
            w32[pl.ds(pl.multiple_of(z * 16 + r * 8, 8), 8), :] = wn[
                pl.ds(z * 16 + r, 8, stride=2), :
            ]

    @pl.loop(0, 8)
    def _(b):
        waves = w32[pl.ds(pl.multiple_of(b * 64, 64), 64), :]
        for t in range(20):
            if t < 16:
                place = lane + ((t // 2) * 320 + (t % 2) * 128)
            else:
                m = t - 16
                place = jnp.where(lane < 64, lane + (640 * m + 256), lane + (640 * m + 512))
            product = waves * place.astype(F32)
            turns = jnp.floor(product * (1.0 / NLON) + 0.5)
            phase = product - turns * NLON
            size = jnp.abs(phase)
            cosine = quarter_sine((640.0 - size) * (1.0 / 640.0))
            fold = 640.0 - jnp.abs(size - 640.0)
            sine = quarter_sine(jnp.where(phase < 0, fold, -fold) * (1.0 / 640.0))
            pair = jnp.concatenate(
                [cosine.reshape(8, 8, 128), sine.reshape(8, 8, 128)], axis=1
            ).reshape(128, 128)
            trig[pl.ds(pl.multiple_of(b * 128, 128), 128), t * 128:(t + 1) * 128] = (
                pair.astype(BF16)
            )

    leg_copy.wait()
    for r in range(2):
        @pl.loop(0, 10)
        def _(s):
            rows = pl.ds(pl.multiple_of(s * 128, 128), 128)
            for u in range(5):
                leg32[u, rows, :] = leg_v[r, rows, u * 128:(u + 1) * 128].astype(F32)

        @pl.loop(0, 8)
        def _(j):
            for i in range(5):
                for u in range(5):
                    rows = pl.ds(pl.multiple_of(i * 256 + j * 32, 32), 32)
                    legp[r, rows, u * 128:(u + 1) * 128] = leg32[
                        u, pl.ds(j * 5 + i, 32, stride=40), :
                    ].astype(BF16)

    def fields_of(shape, axis):
        row = lax.broadcasted_iota(jnp.int32, shape, axis).astype(F32)
        group = jnp.floor((row + 0.5) * (1.0 / 32.0))
        within = row - 32.0 * group
        field = float(FG) * group + within
        vector = jnp.floor((field + 0.5) * (1.0 / 3.0))
        return within < FG - 0.5, vector, field - 3.0 * vector

    used, _, level = fields_of((192, NT), 0)
    wts[...] = jnp.where(
        used,
        jnp.where(
            level < 0.5,
            ew_ref[0:1, :],
            jnp.where(level < 1.5, ew_ref[1:2, :], ew_ref[2:3, :]),
        ),
        0.0,
    )

    def analyse(c):
        first, count = CHUNKS[c]
        window = xa.at[pl.ds(first * 128, count * 128), pl.ds(0, 1792)]
        pltpu.make_async_copy(window, window, s1_recv.at[c]).wait()
        window = xrr.at[pl.ds(0, 7), pl.ds(first * 64, count * 64)]
        pltpu.make_async_copy(window, window, s1r_recv.at[c]).wait()
        own_copy(c).wait()
        for g in range(first, first + count):
            for m in range(4):
                even = xrr[2 * m, g * 64:(g + 1) * 64, :].astype(F32)
                odd = xrr[2 * m + 1, g * 64:(g + 1) * 64, :].astype(F32)
                cols = slice(2048 + m * 128, 2176 + m * 128)
                xa[g * 128:g * 128 + 64, cols] = jnp.where(
                    low, even, pltpu.roll(odd, 64, 1)
                ).astype(BF16)
                xa[g * 128 + 64:g * 128 + 128, cols] = jnp.where(
                    low, pltpu.roll(even, 64, 1), odd
                ).astype(BF16)

        @pl.loop(0, 2)
        def _(h):
            half = lax.rem(lat // 16 + 1 + h, 2)
            rows = pl.ds(pl.multiple_of(half * 512, 512), 512)
            product = nt_dot(trig[rows, :], xa[first * 128:(first + count) * 128, :])
            product = (product * (1.0 / math.sqrt(NLON))).astype(BF16)
            for g in range(count):
                sb[first + g, pl.ds(half * 16, 16)] = product[
                    :, g * 128:(g + 1) * 128
                ].reshape(16, 32, 128)

            @pl.loop(0, 16)
            def _(k):
                peer = half * 16 + lax.rem(lat + k + 8, 16)

                @pl.when(peer != lat)
                def _():
                    pltpu.make_async_remote_copy(
                        src_ref=sb.at[pl.ds(first, count), peer],
                        dst_ref=zb.at[pl.ds(first, count), lat],
                        send_sem=zy_send, recv_sem=zy_recv.at[c],
                        device_id=(peer, lon), device_id_type=MESH,
                    ).start()

        for g in range(first, first + count):
            zb[g, lat] = sb[g, lat]

    def deliver(c):
        first, count = CHUNKS[c]
        window = sb.at[pl.ds(first, count), pl.ds(0, 31)]
        pltpu.make_async_copy(window, window, zy_recv.at[c]).wait()
        for g in range(first, first + count):
            @pl.loop(0, 8)
            def _(s):
                for e in range(4):
                    rows = zb[g, s * 4 + e].astype(F32)
                    for rp in range(4):
                        r32[pl.ds(s * 16 + e * 4 + rp, 8, stride=136), :] = rows[
                            rp * 8:(rp + 1) * 8
                        ]

            for j in range(8):
                rbs[g, j] = r32[j * 136:j * 136 + 128, :].astype(BF16)

        @pl.loop(1, 8)
        def _(k):
            peer = lax.rem(lon + k, 8)
            pltpu.make_async_remote_copy(
                src_ref=rbs.at[pl.ds(first, count), peer],
                dst_ref=rb.at[pl.ds(first, count), lon],
                send_sem=s2_send, recv_sem=s2_recv.at[c],
                device_id=(lat, peer), device_id_type=MESH,
            ).start()

        for g in range(first, first + count):
            rb[g, lon] = rbs[g, lon]

    slot = (lat * 8 + lon) * 2

    def collect(c):
        first, count = CHUNKS[c]
        window = rb.at[pl.ds(first, count), pl.ds(0, 7)]
        pltpu.make_async_copy(window, window, s2_recv.at[c]).wait()
        for g in range(first, first + count):
            @pl.loop(0, 8)
            def _(j):
                c32[pl.ds(pl.multiple_of(j * 128, 128), 128), :] = rb[g, j].astype(F32)

            for r in range(2):
                for p in range(2):
                    ext32[0:128, :] = jnp.transpose(c32[pl.ds(r * 2 + p, 256, stride=4), :])
                    for i in range(5):
                        amat[r, p, g * 32:(g + 1) * 32, i * 256:(i + 1) * 256] = ext32[
                            FG * i:FG * i + 32, :
                        ].astype(BF16)
        rows = slice(first * 32, (first + count) * 32)
        degree = lax.broadcasted_iota(jnp.int32, (count * 64, NT), 1)
        for r in range(2):
            full = jnp.dot(
                amat[r, :, rows, :].reshape(count * 64, 1280), legp[r],
                preferred_element_type=F32,
            )
            full = jnp.where(degree >= wave_ref[slot + r], full, 0.0)
            for p in range(2):
                part = full[p * count * 32:(p + 1) * count * 32]
                out[r, p, rows, :] = part
                for g in range(count):
                    start = 4 * FG * (first + g) + r * 2 + p
                    for u in range(5):
                        ost[u, pl.ds(start, 32, stride=4), :] = part[
                            g * 32:(g + 1) * 32, u * 128:(u + 1) * 128
                        ]

    analyse(0)
    analyse(1)
    analyse(2)
    analyse(3)
    deliver(0)
    analyse(4)
    deliver(1)
    deliver(2)
    analyse(5)
    deliver(3)
    collect(0)
    deliver(4)
    collect(1)
    collect(2)
    deliver(5)
    collect(3)
    collect(4)
    collect(5)

    total = jnp.zeros((192, 192), F32)
    for r in range(2):
        factor = jnp.where(wave_ref[slot + r] == 0, 1.0, 2.0).astype(F32)
        for p in range(2):
            part = out[r, p]
            total += nt_dot(part.astype(BF16), (part * (wts[...] * factor)).astype(BF16))

    _, _, row_level = fields_of((192, 192), 0)
    _, _, col_level = fields_of((192, 192), 1)
    total = jnp.where(row_level == col_level, total, 0.0)
    vec = lax.broadcasted_iota(jnp.int32, (128, 192), 0).astype(F32)
    used, vector, _ = fields_of((128, 192), 1)
    pick = jnp.where(used & (vector == vec), 1.0, 0.0).astype(F32)
    upper = jnp.where(used & (vector == vec - 64.0), 1.0, 0.0).astype(F32)
    high = lax.Precision.HIGHEST
    half = jnp.dot(pick[0:64], total, preferred_element_type=F32, precision=high)
    packed = nt_dot(half[0:32], pick, high) + nt_dot(half[32:64], upper, high)
    gs[...] = (packed * (1.0 / (LEV * M * NT))).reshape(8, 4, 128)

    def ring(which, src, dst):
        @pl.loop(1, 8)
        def _(k):
            peer = lax.rem(lon + k, 8)
            pltpu.make_async_remote_copy(
                src_ref=src(peer), dst_ref=dst.at[lon],
                send_sem=g_send.at[which], recv_sem=g_recv.at[which],
                device_id=(lat, peer), device_id_type=MESH,
            ).start()

    ring(0, lambda peer: gs.at[peer], ga)
    ga[lon] = gs[lon]
    for u in range(5):
        spec_v[:, :, u * 128:(u + 1) * 128] = ost[u, 0:600, :].reshape(300, 2, 128).astype(BF16)
    store = pltpu.make_async_copy(spec_v, spec_ref, spec_sem)
    store.start()
    pltpu.make_async_copy(ga.at[pl.ds(0, 7)], ga.at[pl.ds(0, 7)], g_recv.at[0]).wait()
    gb[lat] = jnp.sum(ga[...], axis=0)

    @pl.loop(1, 32)
    def _(k):
        peer = lax.rem(lat + 1 + lax.rem(k + 11, 31), 32)
        pltpu.make_async_remote_copy(
            src_ref=gb.at[lat], dst_ref=gb.at[lat],
            send_sem=g_send.at[1], recv_sem=g_recv.at[1],
            device_id=(peer, lon), device_id_type=MESH,
        ).start()

    pltpu.make_async_copy(gb.at[pl.ds(0, 31)], gb.at[pl.ds(0, 31)], g_recv.at[1]).wait()
    gc[lon] = jnp.sum(gb[...], axis=0)
    ring(2, lambda peer: gc.at[lon], gc)
    pltpu.make_async_copy(gc.at[pl.ds(0, 7)], gc.at[pl.ds(0, 7)], g_recv.at[2]).wait()
    packed = gc[...].reshape(32, 128)
    gram_ref[0:32, :] = packed[:, 0:50]
    gram_ref[32:50, :] = packed[0:18, 64:114]

    store.wait()

    window = xa.at[:, pl.ds(0, 1792)]
    pltpu.make_async_copy(window, window, s1_send).wait()
    window = xrr.at[pl.ds(0, 7)]
    pltpu.make_async_copy(window, window, s1r_send).wait()
    window = sb.at[:, pl.ds(0, 31)]
    pltpu.make_async_copy(window, window, zy_send).wait()
    window = rb.at[:, pl.ds(0, 7)]
    pltpu.make_async_copy(window, window, s2_send).wait()
    pltpu.make_async_copy(ga.at[pl.ds(0, 7)], ga.at[pl.ds(0, 7)], g_send.at[0]).wait()
    pltpu.make_async_copy(gb.at[pl.ds(0, 31)], gb.at[pl.ds(0, 31)], g_send.at[1]).wait()
    pltpu.make_async_copy(gc.at[pl.ds(0, 7)], gc.at[pl.ds(0, 7)], g_send.at[2]).wait()


def hand_on(spec_in, gram_in, spec_out, gram_out, sems):
    copies = [
        pltpu.make_async_copy(gram_in, gram_out, sems.at[3]),
    ] + [
        pltpu.make_async_copy(
            spec_in.at[pl.ds(100 * b, 100)], spec_out.at[pl.ds(100 * b, 100)], sems.at[b]
        )
        for b in range(3)
    ]
    for copy in copies:
        copy.start()
    for copy in copies:
        copy.wait()


def on_device(grid_fields, legendre, wave_of_slot, energy_weight):
    rows = grid_fields.transpose(1, 2, 0, 3).reshape(150, 40, 320)
    waves = wave_of_slot.reshape(4, 128)
    vmem = pl.BlockSpec(memory_space=pltpu.VMEM)
    dma = pltpu.SemaphoreType.DMA
    many = dma((len(CHUNKS),))
    spectral, gram_matrix = pl.pallas_call(
        kernel,
        out_shape=(
            jax.ShapeDtypeStruct((300, 2, NT), BF16),
            jax.ShapeDtypeStruct((50, 50), F32),
        ),
        in_specs=[
            pl.BlockSpec(memory_space=pl.ANY),
            pl.BlockSpec(memory_space=pl.ANY),
            vmem,
            pl.BlockSpec(memory_space=pltpu.SMEM),
            vmem,
        ],
        out_specs=(pl.BlockSpec(memory_space=pl.ANY), vmem),
        scratch_shapes=[
            pltpu.VMEM((150, 40, 320), BF16),
            pltpu.VMEM((6, 3, 1008, 128), F32),
            pltpu.VMEM((8, 768, 256), BF16),
            pltpu.VMEM((8, 384, 128), BF16),
            pltpu.VMEM((768, NLON), BF16),
            pltpu.VMEM((8, 384, 128), BF16),
            pltpu.VMEM((1024, NLON), BF16),
            pltpu.VMEM((512, 128), F32),
            pltpu.VMEM((512, 128), F32),
            pltpu.VMEM((6, 32, 32, 128), BF16),
            pltpu.VMEM((6, 32, 32, 128), BF16),
            pltpu.VMEM((8 * 136, 128), F32),
            pltpu.VMEM((6, 8, 128, 128), BF16),
            pltpu.VMEM((6, 8, 128, 128), BF16),
            pltpu.VMEM((2, 1280, NT), BF16),
            pltpu.VMEM((5, 1280, 128), F32),
            pltpu.VMEM((2, 1280, NT), BF16),
            pltpu.VMEM((1024, 128), F32),
            pltpu.VMEM((136, 256), F32),
            pltpu.VMEM((2, 2, 192, 1280), BF16),
            pltpu.VMEM((2, 2, 192, NT), F32),
            pltpu.VMEM((5, 632, 128), F32),
            pltpu.VMEM((192, NT), F32),
            pltpu.VMEM((300, 2, NT), BF16),
            pltpu.VMEM((8, 4, 128), F32),
            pltpu.VMEM((8, 4, 128), F32),
            pltpu.VMEM((32, 4, 128), F32),
            pltpu.VMEM((8, 4, 128), F32),
            dma((6,)), dma, dma, many, dma, many, dma, many,
            dma, many, dma, many, dma((3,)), dma((3,)),
        ],
        compiler_params=pltpu.CompilerParams(
            collective_id=0, has_side_effects=True, vmem_limit_bytes=60 * 1024 * 1024,
        ),
        cost_estimate=pl.CostEstimate(
            flops=6_000_000_000, bytes_accessed=12_000_000, transcendentals=0
        ),
    )(rows, legendre, waves, wave_of_slot, energy_weight)
    anywhere = pl.BlockSpec(memory_space=pl.ANY)
    spectral, gram_matrix = pl.pallas_call(
        hand_on,
        out_shape=(
            jax.ShapeDtypeStruct((300, 2, NT), BF16),
            jax.ShapeDtypeStruct((50, 50), F32),
        ),
        in_specs=[vmem, vmem],
        out_specs=(anywhere, anywhere),
        scratch_shapes=[dma((4,))],
    )(spectral, gram_matrix)
    return spectral.reshape(50, LEV, 2, 2, NT), gram_matrix


def solution(mesh):
    placed = (P("lat", None, None, "lon"), P(("lat", "lon"), None, None), P(), P())
    return jax.shard_map(
        on_device,
        mesh=mesh,
        in_specs=placed,
        out_specs=(P(None, None, ("lat", "lon"), None, None), P()),
        check_vma=False,
    )
```

profile of v0, /device:TPU:1, one launch (start us, length us, event | category | flops | bytes accessed | tf_op | source)
XLA Modules:
  0.0 91.8 jit_solution(7740232493012051206)
XLA Ops:
  0.6 89.1 %shard_map.59 = (bf16[300,2,640]{2,1,0:T(2,128)(2,1)}, f32[50,50]{1,0:T(8,128)}) custom-call(bf16[150,40,320]{2,1,0:T(8,128)(2,1)} %bitcast.5, bf16[2,1280,640]{2,1,0:T(8,128)(2,1)} %leg_hbm.1, s32[4,128]{1,0:T(4,128)} %bitcast.7, s32[512]{0:T(512)} %wave_ref.1, f32[3,640]{1,0:T(4,128)} %ew_ref.1), custom_call_target="tpu_custom_call" | custom-call | flops 6000000000 | bytes 12000000 | tf_op jit(solution)/shard_map/pallas_call | solution.py:441
  89.8 2.0 %shard_map.60 = (bf16[300,2,640]{2,1,0:T(2,128)(2,1)}, f32[50,50]{1,0:T(8,128)}) custom-call(bf16[300,2,640]{2,1,0:T(2,128)(2,1)} %get-tuple-element.6.spec_in, f32[50,50]{1,0:T(8,128)} %get-tuple-element.7.gram_in), custom_call_target="tpu_custom_call" | custom-call | tf_op jit(solution)/shard_map/pallas_call | solution.py:495
where the time goes:
time: 92 us; the launch traced here: 91.8 us
  Pallas kernels  91.2 us (99%)
    pallas_call x1, Pallas kernels, on_device(): pl.pallas_call(kernel, out_shape=(jax.ShapeDtypeStruct((300, 2, NT), BF16...  89.1 us
    pallas_call x1, Pallas kernels, on_device(): pl.pallas_call(hand_on, out_shape=(jax.ShapeDtypeStruct((300, 2, NT), BF1...  2.04 us

commit v1 on v0

--- a/solution.py
+++ b/solution.py
@@ -39,7 +39,7 @@
 def kernel(
     x_hbm, leg_hbm, wq_ref, wave_ref, ew_ref, spec_ref, gram_ref,
     xv, x32, xs, xrs, xa, xrr, trig, wn, w32, sb, zb, r32, rbs, rb, leg_v, leg32, legp,
-    c32, ext32, amat, out, ost, wts, spec_v, gs, ga, gb, gc,
+    c32, ext32, amat, out, ost, wts, same, picks, spec_v, gs, ga, gb, gc,
     x_sem, leg_sem, spec_sem, own_sem, s1_send, s1_recv, s1r_send, s1r_recv,
     zy_send, zy_recv, s2_send, s2_recv, g_send, g_recv,
 ):
@@ -215,6 +215,14 @@
         ),
         0.0,
     )
+
+    _, _, row_level = fields_of((192, 192), 0)
+    _, _, col_level = fields_of((192, 192), 1)
+    same[...] = jnp.where(row_level == col_level, 1.0, 0.0)
+    vec = lax.broadcasted_iota(jnp.int32, (128, 192), 0).astype(F32)
+    used, vector, _ = fields_of((128, 192), 1)
+    picks[0] = jnp.where(used & (vector == vec), 1.0, 0.0).astype(F32)
+    picks[1] = jnp.where(used & (vector == vec - 64.0), 1.0, 0.0).astype(F32)
 
     def analyse(c):
         first, count = CHUNKS[c]
@@ -354,13 +362,9 @@
             part = out[r, p]
             total += nt_dot(part.astype(BF16), (part * (wts[...] * factor)).astype(BF16))
 
-    _, _, row_level = fields_of((192, 192), 0)
-    _, _, col_level = fields_of((192, 192), 1)
-    total = jnp.where(row_level == col_level, total, 0.0)
-    vec = lax.broadcasted_iota(jnp.int32, (128, 192), 0).astype(F32)
-    used, vector, _ = fields_of((128, 192), 1)
-    pick = jnp.where(used & (vector == vec), 1.0, 0.0).astype(F32)
-    upper = jnp.where(used & (vector == vec - 64.0), 1.0, 0.0).astype(F32)
+    total = jnp.where(same[...] > 0.5, total, 0.0)
+    pick = picks[0]
+    upper = picks[1]
     high = lax.Precision.HIGHEST
     half = jnp.dot(pick[0:64], total, preferred_element_type=F32, precision=high)
     packed = nt_dot(half[0:32], pick, high) + nt_dot(half[32:64], upper, high)
@@ -476,6 +480,8 @@
             pltpu.VMEM((2, 2, 192, NT), F32),
             pltpu.VMEM((5, 632, 128), F32),
             pltpu.VMEM((192, NT), F32),
+            pltpu.VMEM((192, 192), F32),
+            pltpu.VMEM((2, 128, 192), F32),
             pltpu.VMEM((300, 2, NT), BF16),
             pltpu.VMEM((8, 4, 128), F32),
             pltpu.VMEM((8, 4, 128), F32),

time: 92 us -> 92 us (level)
  no operation moved by 1% of the time
where the time goes in v1:
time: 92 us; the launch traced here: 91.8 us
  Pallas kernels  91.2 us (99%)
    pallas_call x1, Pallas kernels, on_device(): pl.pallas_call(kernel, out_shape=(jax.ShapeDtypeStruct((300, 2, NT), BF16...  89.1 us
    pallas_call x1, Pallas kernels, on_device(): pl.pallas_call(hand_on, out_shape=(jax.ShapeDtypeStruct((300, 2, NT), BF1...  2.04 us

profile of v1, /device:TPU:1, one launch (start us, length us, event | category | flops | bytes accessed | tf_op | source)
XLA Modules:
  0.0 91.8 jit_solution(7647819369264368698)
XLA Ops:
  0.6 89.1 %shard_map.59 = (bf16[300,2,640]{2,1,0:T(2,128)(2,1)}, f32[50,50]{1,0:T(8,128)}) custom-call(bf16[150,40,320]{2,1,0:T(8,128)(2,1)} %bitcast.5, bf16[2,1280,640]{2,1,0:T(8,128)(2,1)} %leg_hbm.1, s32[4,128]{1,0:T(4,128)} %bitcast.7, s32[512]{0:T(512)} %wave_ref.1, f32[3,640]{1,0:T(4,128)} %ew_ref.1), custom_call_target="tpu_custom_call" | custom-call | flops 6000000000 | bytes 12000000 | tf_op jit(solution)/shard_map/pallas_call | solution.py:445
  89.8 2.0 %shard_map.60 = (bf16[300,2,640]{2,1,0:T(2,128)(2,1)}, f32[50,50]{1,0:T(8,128)}) custom-call(bf16[300,2,640]{2,1,0:T(2,128)(2,1)} %get-tuple-element.6.spec_in, f32[50,50]{1,0:T(8,128)} %get-tuple-element.7.gram_in), custom_call_target="tpu_custom_call" | custom-call | tf_op jit(solution)/shard_map/pallas_call | solution.py:501
